TPU v7x, 256 devices: a whole 4x4x8 slice. The times are simulated.
256 devices in a mesh: cfg: 2 (over core), patch: 16 (over z, y_hi), tensor: 8 (over y_lo, x).
Axes of the slice: x: 4, y: 4 (y_hi: 2, y_lo: 2; y = y_hi * 2 + y_lo), z: 8, core: 2. Of those that a mesh axis runs over, the one named last changes fastest.
Arguments:
- hidden: bfloat16 [2, 2048, 3072], P('cfg', ('patch', 'tensor')), may hold values from -6 to 6
- stale_kv: bfloat16 [2, 2, 2048, 3072], P('cfg', None, 'patch', 'tensor'), may hold values from -80 to 80
- w_qkv: bfloat16 [3072, 3, 3072], P(None, None, 'tensor'), may hold values from -0.109375 to 0.109375
- w_out: bfloat16 [3072, 3072], P('tensor'), may hold values from -0.4375 to 0.4375
- mod_table: float32 [32, 3, 3072], replicated, may hold values from -5 to 5
- segment_ids: int32 [2048], replicated, may hold values from 0 to 7, never falling along the last dimension, each value on 1 to 1152 neighbouring positions
- step_index: int32 [8], replicated, may hold values from 0 to 31
- guide_scale: float32 [8], replicated, may hold values from 1.5 to 4
Outputs:
- branch_out: bfloat16 [2, 2048, 3072], P('cfg', ('patch', 'tensor'))
- guided: bfloat16 [2048, 3072], P(('patch', 'tensor'), 'cfg')
Inputs may be any that keep to these rules, and one draw needn't show every extreme that they name: `segment_ids`: request ids never fall along the sequence; every request is present with 1 to 1152 tokens, one request exactly that many.
All inputs are finite; a program needn't handle non-finite values.
Results may differ from a plain program's by a relative error of at most 0.029.
Values may be sent and summed in bfloat16 or wider, within the bound.
A program may use at most 64 MiB of HBM per device.

v0:
```python
import math

import jax
import jax.numpy as jnp
from jax import lax
from jax.sharding import PartitionSpec as P

HEAD_DIM = 128


def from_partner(array, axis, apart):
    return lax.ppermute(array, axis, [(i, i ^ 1 << apart) for i in range(lax.axis_size(axis))])


def body(hidden, stale_kv, w_qkv, w_out, mod_table, segment_ids, step_index, guide_scale):
    row_count = hidden.shape[1]
    model_width = hidden.shape[2]
    slab_rows = stale_kv.shape[2]
    local_width = w_qkv.shape[2]
    heads_here = local_width // HEAD_DIM
    table_rows = mod_table.shape[0]
    requests = step_index.shape[0]
    tensor_pos = lax.axis_index("tensor")
    patch_pos = lax.axis_index("patch")
    branch_pos = lax.axis_index("cfg")
    highest = lax.Precision.HIGHEST
    pick_step = (step_index[:, None] == jnp.arange(table_rows, dtype=jnp.int32)[None, :]).astype(
        jnp.float32
    )
    request_mods = jnp.dot(
        pick_step, mod_table.reshape(table_rows, 3 * model_width), precision=highest
    )
    slab_begin = patch_pos * slab_rows
    slab_segments = lax.dynamic_slice_in_dim(segment_ids, slab_begin, slab_rows, 0)
    own_segments = lax.dynamic_slice_in_dim(
        segment_ids, slab_begin + tensor_pos * row_count, row_count, 0
    )
    pick_request = (own_segments[:, None] == jnp.arange(requests, dtype=jnp.int32)[None, :]).astype(
        jnp.float32
    )
    token_mods = jnp.dot(pick_request, request_mods, precision=highest)
    shift_mod = token_mods[:, :model_width]
    scale_mod = token_mods[:, model_width : 2 * model_width]
    gate_mod = token_mods[:, 2 * model_width :]
    residual_in = hidden[0].astype(jnp.float32)
    row_mean = jnp.mean(residual_in, axis=-1, keepdims=True)
    row_var = jnp.mean((residual_in - row_mean) ** 2, axis=-1, keepdims=True)
    normed = (residual_in - row_mean) / jnp.sqrt(row_var + 1e-06)
    modulated = (normed * (1.0 + scale_mod) + shift_mod).astype(jnp.bfloat16)
    weights_flat = w_qkv.reshape(model_width, 3 * local_width)
    fresh = jnp.dot(
        lax.all_gather(modulated, "tensor", axis=0, tiled=True),
        weights_flat,
        preferred_element_type=jnp.float32,
    ).astype(jnp.bfloat16)
    fresh = fresh.reshape(slab_rows, 3, heads_here, HEAD_DIM)
    queries = jnp.transpose(fresh[:, 0], (1, 0, 2))
    factor = 1.0 / HEAD_DIM**0.5

    def absorb(carry_state, key_block, value_block, allowed):
        running_max, running_sum, weighted = carry_state
        scores = (
            jnp.einsum("hqd,khd->hqk", queries, key_block, preferred_element_type=jnp.float32)
            * factor
        )
        scores = jnp.where(allowed[None], scores, -1e30)
        new_max = jnp.maximum(running_max, jnp.max(scores, axis=2))
        soft_weights = jnp.where(allowed[None], jnp.exp(scores - new_max[..., None]), 0.0)
        shrink = jnp.exp(running_max - new_max)
        running_sum = running_sum * shrink + jnp.sum(soft_weights, axis=2)
        weighted = weighted * shrink[..., None] + jnp.einsum(
            "hqk,khd->hqd",
            soft_weights.astype(jnp.bfloat16),
            value_block,
            preferred_element_type=jnp.float32,
        )
        return (new_max, running_sum, weighted)

    initial = (
        jnp.full((heads_here, slab_rows), -1e30, jnp.float32),
        jnp.zeros((heads_here, slab_rows), jnp.float32),
        jnp.zeros((heads_here, slab_rows, HEAD_DIM), jnp.float32),
    )
    own_allowed = slab_segments[:, None] == slab_segments[None, :]
    carry_state = absorb(initial, fresh[:, 1], fresh[:, 2], own_allowed)
    key_rows = lax.all_gather(stale_kv[0, 0], "patch", axis=0, tiled=True)
    value_rows = lax.all_gather(stale_kv[0, 1], "patch", axis=0, tiled=True)
    piece_rows = key_rows.shape[0]
    block_rows = math.gcd(piece_rows, 1024)
    block_count = piece_rows // block_rows
    key_blocks = key_rows.reshape(block_count, block_rows, heads_here, HEAD_DIM)
    value_blocks = value_rows.reshape(block_count, block_rows, heads_here, HEAD_DIM)
    segment_blocks = segment_ids.reshape(block_count, block_rows)
    positions = jnp.arange(piece_rows, dtype=jnp.int32).reshape(block_count, block_rows)

    def block_step(state_in, block_data):
        key_part, value_part, segment_part, position = block_data
        outside = (position < slab_begin) | (position >= slab_begin + slab_rows)
        allowed = (slab_segments[:, None] == segment_part[None, :]) & outside[None, :]
        state_out = absorb(state_in, key_part, value_part, allowed)
        return (state_out, None)

    result_state, trailing = lax.scan(
        block_step, carry_state, (key_blocks, value_blocks, segment_blocks, positions)
    )
    running_max, running_sum, weighted = result_state
    attn = jnp.transpose(weighted / running_sum[..., None], (1, 0, 2)).reshape(
        slab_rows, local_width
    )
    attn = attn.astype(jnp.bfloat16)
    everything = lax.psum(
        jnp.dot(attn, w_out, preferred_element_type=jnp.float32).astype(jnp.bfloat16), "tensor"
    ).astype(jnp.float32)
    projected = lax.dynamic_slice_in_dim(everything, tensor_pos * row_count, row_count, 0)
    branch_rows = (residual_in + gate_mod * projected).astype(jnp.bfloat16)
    half_width = model_width // 2
    other_half = lax.dynamic_slice_in_dim(branch_rows, (1 - branch_pos) * half_width, half_width, 1)
    own_half = lax.dynamic_slice_in_dim(branch_rows, branch_pos * half_width, half_width, 1)
    partner = from_partner(other_half, "cfg", 0)
    is_first = branch_pos == 0
    conditional = jnp.where(is_first, own_half, partner).astype(jnp.float32)
    unconditional = jnp.where(is_first, partner, own_half).astype(jnp.float32)
    strength = jnp.dot(pick_request, guide_scale[:, None], precision=highest)
    guided = (unconditional + strength * (conditional - unconditional)).astype(jnp.bfloat16)
    return (branch_rows[None], guided)


def solution(mesh):
    placed = (
        P("cfg", ("patch", "tensor"), None),
        P("cfg", None, "patch", "tensor"),
        P(None, None, "tensor"),
        P("tensor", None),
        P(),
        P(),
        P(),
        P(),
    )
    return jax.shard_map(
        body,
        mesh=mesh,
        in_specs=placed,
        out_specs=(P("cfg", ("patch", "tensor"), None), P(("patch", "tensor"), "cfg")),
        check_vma=False,
    )
```

profile of v0, /device:TPU:1, one launch (start us, length us, event | category | flops | bytes accessed | tf_op | source)
XLA Modules:
  0.0 282.3 jit_solution(3439421499853925229)
XLA Ops:
  7.2 1.8 fusion.41
  9.1 0.7 all-gather.7.cloned.1.call-update
  9.9 1.4 copy.37
  11.4 0.7 fusion.18
  12.2 0.5 fusion.34
  12.7 0.4 fusion.31
  13.3 10.3 %copy.17 = bf16[3072,3,384]{0,2,1:T(8,128)(2,1)} copy(bf16[3072,3,384]{2,0,1:T(8,128)(2,1)} %param.12) | data formatting | bytes 14155776 | tf_op args[2]
  23.7 25.4 %all_gather.9 = bf16[128,3072]{1,0:T(8,128)(2,1)S(1)} all-gather(bf16[16,3072]{1,0:T(8,128)(2,1)S(1)} %fusion.22), channel_id=1, replica_groups=mesh['cfg'=2,'patch'=16,'tensor'=8] {'tensor'}, dimensions={0}, use_global_device_ids=true | all-gather | bytes 884736 | tf_op jit(solution)/shard_map/all_gather | solution.py:52
  49.1 5.4 %convolution_convert_fusion.1 = bf16[128,1152]{1,0:T(8,128)(2,1)S(1)} fusion(bf16[128,3072]{1,0:T(8,128)(2,1)S(1)} %all_gather.9, bf16[3072,1152]{0,1:T(8,128)(2,1)} %bitcast.80), kind=kOutput, calls=%fused_computation.21 | convolution fusion | flops 906117120 | bytes 8159232 | tf_op jit(solution)/shard_map/dot_general | solution.py:51
  54.4 0.9 copy.18
  55.3 0.9 slice.35
  56.5 1.1 fusion.42
  57.8 1.1 convolution_add_fusion.1
  58.9 34.3 %all-gather.5.cloned.1.call-done = bf16[1,1,2048,384]{3,2,1,0:T(8,128)(2,1)} async-done(((bf16[1,1,128,384]{3,2,1,0:T(8,128)(2,1)}), bf16[1,1,2048,384]{3,2,1,0:T(8,128)(2,1)}) %all-gather.5.cloned.1.call-update) | async-done | bytes 1572880 | tf_op jit(solution)/shard_map/all_gather | solution.py:86
  93.2 5.1 %reshape.149 = bf16[2,1024,3,128]{3,2,1,0:T(4,128)(2,1)} reshape(bf16[1,1,2048,384]{3,2,1,0:T(8,128)(2,1)} %all-gather.5.cloned.1.call-done) | data formatting | bytes 3145728 | tf_op jit(solution)/shard_map/reshape | solution.py:91
  98.3 3.0 %copy.25 = bf16[2,1024,3,128]{3,1,2,0:T(8,128)(2,1)} copy(bf16[2,1024,3,128]{3,2,1,0:T(4,128)(2,1)} %reshape.149) | data formatting | bytes 3145728 | tf_op jit(solution)/shard_map/while | solution.py:103
  101.3 74.0 %all-gather.7.cloned.1.call-done = bf16[1,1,2048,384]{3,2,1,0:T(8,128)(2,1)} async-done(((bf16[1,1,128,384]{3,2,1,0:T(8,128)(2,1)}), bf16[1,1,2048,384]{3,2,1,0:T(8,128)(2,1)}) %all-gather.7.cloned.1.call-update) | async-done | bytes 1572880 | tf_op jit(solution)/shard_map/all_gather | solution.py:87
  175.2 5.1 %reshape.150 = bf16[2,1024,3,128]{3,2,1,0:T(4,128)(2,1)} reshape(bf16[1,1,2048,384]{3,2,1,0:T(8,128)(2,1)} %all-gather.7.cloned.1.call-done) | data formatting | bytes 3145728 | tf_op jit(solution)/shard_map/reshape | solution.py:92
  180.4 3.0 %copy.26 = bf16[2,1024,3,128]{3,1,2,0:T(8,128)(2,1)} copy(bf16[2,1024,3,128]{3,2,1,0:T(4,128)(2,1)} %reshape.150) | data formatting | bytes 3145728 | tf_op jit(solution)/shard_map/while | solution.py:103
  183.3 6.1 %while.15 = (s32[]{:T(128)}, f32[3,128]{1,0:T(4,128)S(1)}, f32[3,128]{1,0:T(4,128)S(1)}, f32[3,128,128]{2,1,0:T(8,128)S(1)}, s32[128]{0:T(128)S(1)}, /*index=5*/...) while((s32[]{:T(128)}, f32[3,128]{1,0:T(4,128)S(1)}, ...), condition=%wide.region_7.8_spmd, body=%wide.region_4.7_spmd.sunk | while | flops 205229824 | bytes 13643949 | solution.py:103
  183.4 0.3 compare_and_fusion.2
  183.7 1.7 fusion.58
  185.8 0.6 convolution_add_fusion.3
  186.4 0.3 compare_and_fusion.2
  186.8 1.7 fusion.58
  188.8 0.6 convolution_add_fusion.3
  189.7 1.5 convolution_convert_fusion
  191.2 76.3 %all-reduce.2.cloned.1.call-done = bf16[128,3072]{1,0:T(8,128)(2,1)} async-done(((bf16[128,3072]{1,0:T(8,128)(2,1)}), bf16[128,3072]{1,0:T(8,128)(2,1)}) %all-reduce.2.cloned.1.call-update) | async-done | bytes 786448 | tf_op jit(solution)/shard_map/psum | solution.py:111
  267.5 0.9 fusion.21
  268.5 5.7 %collective-permute-start = (bf16[16,1536]{1,0:T(8,128)(2,1)S(1)}, bf16[16,1536]{1,0:T(8,128)(2,1)S(1)}, u32[]{:S(2)}, u32[]{:S(2)}) collective-permute-start(bf16[16,1536]{1,0:T(8,128)(2,1)S(1)} %constant_dynamic-slice_fusion.1), channel_id=1, source_target_pairs={{0,128},{128,0},{1,129},{129,1},{2,130},{130,2},{3,131},{131,3},{4... | collective-permute-start | bytes 147464 | tf_op jit(solution)/shard_map/ppermute | solution.py:12
  274.4 0.7 collective-permute-done
  275.1 0.7 fusion.26
  (62 shorter events, 2.0 us)
Async XLA Ops:
  7.2 182.5 %copy-start = (bf16[384,3072]{1,0:T(8,128)(2,1)S(1)}, bf16[384,3072]{1,0:T(8,128)(2,1)}, u32[]{:S(2)}) copy-start(bf16[384,3072]{1,0:T(8,128)(2,1)} %param.13) | copy-start | bytes 7077892
  7.2 5.0 %copy-start.5 = (s32[2048]{0:T(1024)S(1)}, s32[2048]{0:T(1024)}, u32[]{:S(2)}) copy-start(s32[2048]{0:T(1024)} %param.15) | copy-start | bytes 24580
  7.2 5.0 %copy-start.8 = (s32[8]{0:T(128)S(1)}, s32[8]{0:T(128)}, u32[]{:S(2)}) copy-start(s32[8]{0:T(128)} %param.16) | copy-start | bytes 100
  7.2 86.0 %all-gather.5.cloned.1.call-start = ((), (), s32[]{:S(2)}) async-start(), calls=%async_computation.1 | async-start | bytes 1671168 | tf_op jit(solution)/shard_map/all_gather | solution.py:86
  9.0 166.2 %all-gather.7.cloned.1.call-start = ((), (), s32[]{:S(2)}) async-start(), calls=%async_computation.2 | async-start | bytes 1671168 | tf_op jit(solution)/shard_map/all_gather | solution.py:87
  9.8 257.7 %all-reduce.2.cloned.1.call-start = ((), (), s32[]{:S(2)}) async-start(), calls=%async_computation | async-start | bytes 1572864 | tf_op jit(solution)/shard_map/psum | solution.py:111
  9.9 1.4 copy-start.2
  11.4 1.8 copy-start.6
  12.2 1.1 copy-start.11
  12.2 1.0 copy-start.9
  13.2 10.3 %copy-start.3 = (bf16[1,16,3072]{2,1,0:T(8,128)(2,1)S(1)}, bf16[1,16,3072]{2,1,0:T(8,128)(2,1)}, u32[]{:S(2)}) copy-start(bf16[1,16,3072]{2,1,0:T(8,128)(2,1)} %param.10) | copy-start | bytes 294916
  13.3 10.3 %copy-start.7 = (f32[16]{0:T(128)S(1)}, f32[16]{0:T(128)}, u32[]{:S(2)}) copy-start(f32[16]{0:T(128)} %copy-done.6) | copy-start | bytes 196
  183.7 2.0 copy-start.1
  186.8 2.0 copy-start.1
  189.6 84.6 %copy-start.10 = (s32[16]{0:T(128)S(1)}, s32[16]{0:T(128)}, u32[]{:S(2)}) copy-start(s32[16]{0:T(128)} %copy-done.9) | copy-start | bytes 196
  189.6 84.6 %copy-start.12 = (f32[8]{0:T(128)S(1)}, f32[8]{0:T(128)}, u32[]{:S(2)}) copy-start(f32[8]{0:T(128)} %param.17) | copy-start | bytes 100
  268.4 7.3 %copy-start.4 = (bf16[16,3072]{1,0:T(8,128)(2,1)}, bf16[16,3072]{1,0:T(8,128)(2,1)S(1)}, u32[]{:S(2)}) copy-start(bf16[16,3072]{1,0:T(8,128)(2,1)S(1)} %fusion.21) | copy-start | bytes 294916
  268.5 6.6 %collective-permute-start = (bf16[16,1536]{1,0:T(8,128)(2,1)S(1)}, bf16[16,1536]{1,0:T(8,128)(2,1)S(1)}, u32[]{:S(2)}, u32[]{:S(2)}) collective-permute-start(bf16[16,1536]{1,0:T(8,128)(2,1)S(1)} %constant_dynamic-slice_fusion.1), channel_id=1, source_target_pairs={{0,128},{128,0},{1,129},{129,1},{2,130},{130,2},{3,131},{131,3},{4... | collective-permute-start | bytes 147464 | tf_op jit(solution)/shard_map/ppermute | solution.py:12
Sparse Core Ops, SparseCore 0:
  10.6 82.4 all-gather.4
  96.3 78.8 all-gather.6
  191.3 76.1 all-reduce.1
where the time goes:
time: 283 us; the launch traced here: 282 us
  waiting for transfers between devices  186 us (66%)
  local copies, waits for them, and re-layouts  31.9 us (11%)
  blocking collectives  25.4 us (9%)
  matrix products  14.9 us (5%)
  between operations  14 us (5%)
  starting transfers between devices  5.84 us (2%)
  other arithmetic  4.2 us (1%)
    psum x1, waiting for transfers between devices, body(): lax.psum(jnp.dot(attn, w_out, preferred_element_type=jnp.float32).astype(...  76.3 us
    all_gather x1, waiting for transfers between devices, body(): value_rows = lax.all_gather(stale_kv[0, 1], 'patch', axis=0, tiled=True)  74 us
    all_gather x1, waiting for transfers between devices, body(): key_rows = lax.all_gather(stale_kv[0, 0], 'patch', axis=0, tiled=True)  34.3 us
    all_gather x1, blocking collectives, body(): lax.all_gather(modulated, 'tensor', axis=0, tiled=True)  25.4 us
    unnamed x26, local copies, waits for them, and re-layouts  10.5 us
    while x3, local copies, waits for them, and re-layouts, body(): lax.scan(block_step, carry_state, (key_blocks, value_blocks, segment_bloc...  6.07 us
    ppermute x1, starting transfers between devices, from_partner(): lax.ppermute(array, axis, [(i, i ^ 1 << apart) for i in range(lax.axis_si...  5.72 us
  transfers between devices with their start and end apart: 4, of which 4 were waited for; matrix products, arithmetic and copies ran while one was open for 11% of the time, Pallas kernels for 0%

commit v1 on v0

v1 whole, which is shorter than its diff:
```python
import functools
import math

import jax
import jax.numpy as jnp
from jax import lax
from jax.experimental import pallas as pl
from jax.experimental.pallas import tpu as pltpu
from jax.sharding import PartitionSpec as P

MESH = pl.DeviceIdType.MESH
HEAD_DIM = 128
NZ = 8
NX = 4
NT = 8
NP = 16
KEY, VAL = 0, 1
NEG = -1e30


def slot_of(d, e):
    return (d % NZ) * 2 + e


FORWARD = {}
for _h in (KEY, VAL):
    FORWARD[(0, 0, _h)] = [("z+", -1, 0), ("z-", 1, 0), ("y", 0, 1)]
    FORWARD[(-1, 0, _h)] = [("z+", -2, 0), ("y", -1, 1)]
    FORWARD[(1, 0, _h)] = [("z-", 2, 0), ("y", 1, 1)]
    FORWARD[(-2, 0, _h)] = [("z+", -3, 0)]
    FORWARD[(2, 0, _h)] = [("z-", 3, 0)]
    FORWARD[(-3, 0, _h)] = [("y", -3, 1)]
    FORWARD[(3, 0, _h)] = [("y", 3, 1)]
    FORWARD[(-1, 1, _h)] = [("z+", -2, 1)]
    FORWARD[(1, 1, _h)] = [("z-", 2, 1)]
FORWARD[(-3, 0, KEY)].append(("z+", 4, 0))
FORWARD[(3, 0, VAL)].append(("z-", 4, 0))
FORWARD[(-3, 1, KEY)] = [("z+", 4, 1)]
FORWARD[(3, 1, VAL)] = [("z-", 4, 1)]
LINKS = {"z+": 0, "z-": 1, "y": 2}


def kernel(
    hidden,
    stale,
    w_qkv,
    w_out,
    mod_table,
    segments,
    steps,
    strengths,
    branch_out,
    guided_out,
    hid,
    mods,
    segs,
    query_segs,
    wq,
    wo,
    tokens,
    kv,
    queries,
    run_max,
    run_sum,
    mixed,
    attn,
    partial,
    parts,
    branch,
    partner,
    guided,
    local_sem,
    kv_send,
    kv_recv,
    tok_send,
    tok_recv,
    sum_send,
    sum_recv,
    pair_send,
    pair_recv,
    out_sem,
):
    cfg = lax.axis_index("cfg")
    patch = lax.axis_index("patch")
    tensor = lax.axis_index("tensor")
    z, yh = patch // 2, patch % 2
    yl, x = tensor // NX, tensor % NX
    width = hid.shape[1]
    half = width // 2
    rows = hid.shape[0]
    heads = queries.shape[1] // HEAD_DIM

    def tensor_peer(dx, dy):
        return (cfg, patch, ((yl + dy) % 2) * NX + (x + dx) % NX)

    links = {
        "z+": (cfg, ((z + 1) % NZ) * 2 + yh, tensor),
        "z-": (cfg, ((z + NZ - 1) % NZ) * 2 + yh, tensor),
        "y": (cfg, z * 2 + (1 - yh), tensor),
    }
    core = (1 - cfg, patch, tensor)
    peers = [(dx, dy) for dy in (0, 1) for dx in range(NX) if (dx, dy) != (0, 0)]

    loads = [
        pltpu.make_async_copy(hidden, hid, local_sem.at[0]),
        pltpu.make_async_copy(segments, segs, local_sem.at[1]),
        pltpu.make_async_copy(mod_table, mods, local_sem.at[2]),
        pltpu.make_async_copy(w_qkv, wq, local_sem.at[3]),
        pltpu.make_async_copy(w_out, wo, local_sem.at[4]),
    ]
    for load in loads:
        load.start()

    barrier = pltpu.get_barrier_semaphore()
    greeted = list(links.values()) + [core] + [tensor_peer(dx, dy) for dx, dy in peers]
    for device in greeted:
        pl.semaphore_signal(barrier, inc=1, device_id=device, device_id_type=MESH)

    loads[0].wait()
    residual = hid[...].astype(jnp.float32)
    mean = jnp.sum(residual, axis=-1, keepdims=True) * (1.0 / width)
    centred = residual - mean
    var = jnp.sum(centred * centred, axis=-1, keepdims=True) * (1.0 / width)
    normed = centred * lax.rsqrt(var + 1e-6)
    loads[1].wait()
    own_row = jnp.broadcast_to(segs[pl.ds(patch, 1), :], (NP * 8, NP * 8))
    query_segs[...] = own_row.T
    own_segs = query_segs[pl.ds(pl.multiple_of(tensor * rows, rows), rows), :]
    loads[2].wait()

    def token_mods(which):
        wide = jnp.concatenate([own_segs] * (width // 128), axis=1)
        picked = jnp.zeros((rows, width), jnp.float32)
        for r in range(8):
            row = mods[which, pl.ds(steps[r], 1), :]
            picked = jnp.where(wide == r, row, picked)
        return picked

    own_rows = pl.ds(pl.multiple_of(tensor * rows, rows), rows)
    tokens[own_rows, :] = (normed * (1.0 + token_mods(1)) + token_mods(0)).astype(jnp.bfloat16)

    pl.semaphore_wait(barrier, len(greeted))

    sent = []

    def send(src, dst, send_sem, recv_sem, device):
        copy = pltpu.make_async_remote_copy(
            src_ref=src,
            dst_ref=dst,
            send_sem=send_sem,
            recv_sem=recv_sem,
            device_id=device,
            device_id_type=MESH,
        )
        copy.start()
        sent.append(copy)

    def arrived(dst, recv_sem, send_sem):
        pltpu.make_async_remote_copy(
            src_ref=dst,
            dst_ref=dst,
            send_sem=send_sem,
            recv_sem=recv_sem,
            device_id=core,
            device_id_type=MESH,
        ).wait_recv()

    def token_rows(dx, dy):
        at = (((yl + dy) % 2) * NX + (x + dx) % NX) * rows
        return tokens.at[pl.ds(pl.multiple_of(at, rows), rows), :]

    def send_tokens(dy, dx_to, index):
        block = token_rows(0, dy)
        slot = dy * NX + (-dx_to) % NX
        send(block, block, tok_send.at[index], tok_recv.at[slot], tensor_peer(dx_to, 0))

    def wait_tokens(dx, dy):
        block = token_rows(dx, dy)
        arrived(block, tok_recv.at[dy * NX + dx], tok_send.at[0])

    counter = {"kv": 0}

    def spread(d, e, h):
        src = stale.at[h] if (d, e) == (0, 0) else kv.at[slot_of(d, e), h]
        for link, to_d, to_e in FORWARD.get((d, e, h), ()):
            slot = slot_of(to_d, to_e)
            send(
                src,
                kv.at[slot, h],
                kv_send.at[counter["kv"]],
                kv_recv.at[slot, h],
                links[link],
            )
            counter["kv"] += 1

    def take(d, e, h):
        slot = slot_of(d, e)
        arrived(kv.at[slot, h], kv_recv.at[slot, h], kv_send.at[0])
        spread(d, e, h)

    block = token_rows(0, 0)
    send(block, block, tok_send.at[0], tok_recv.at[NX], tensor_peer(0, 1))
    for index, dx in enumerate((1, NX - 1, 2)):
        send_tokens(0, dx, 1 + index)
    spread(0, 0, KEY)
    spread(0, 0, VAL)
    wait_tokens(0, 1)
    for index, dx in enumerate((1, NX - 1, 2)):
        send_tokens(1, dx, 4 + index)
    for h in (KEY, VAL):
        take(-1, 0, h)
        take(1, 0, h)
    for h in (KEY, VAL):
        take(-2, 0, h)
        take(2, 0, h)
        take(-1, 1, h)
        take(1, 1, h)
    for dx, dy in peers:
        if (dx, dy) != (0, 1):
            wait_tokens(dx, dy)
    loads[3].wait()
    for j in range(3):
        fresh = jnp.dot(tokens[...], wq[j], preferred_element_type=jnp.float32)
        fresh = fresh.astype(jnp.bfloat16)
        if j == 0:
            queries[...] = fresh
        else:
            kv[0, j - 1] = fresh

    scale = math.log2(math.e) / HEAD_DIM**0.5

    def attend(d, e, first=False):
        slot = slot_of(d, e)
        slab = ((z + d) % NZ) * 2 + (yh + e) % 2
        allowed = query_segs[...] == segs[pl.ds(slab, 1), :]
        for head in range(heads):
            cols = slice(head * HEAD_DIM, (head + 1) * HEAD_DIM)
            scores = lax.dot_general(
                queries[:, cols],
                kv[slot, KEY, :, cols],
                (((1,), (1,)), ((), ())),
                preferred_element_type=jnp.float32,
            )
            scores = jnp.where(allowed, scores * scale, NEG)
            top = jnp.max(scores, axis=1, keepdims=True)
            if first:
                new_max = jnp.broadcast_to(top, scores.shape)
            else:
                old_max = run_max[head]
                new_max = jnp.maximum(old_max, top)
            weights = jnp.exp2(scores - new_max)
            product = jnp.dot(
                weights.astype(jnp.bfloat16),
                kv[slot, VAL, :, cols],
                preferred_element_type=jnp.float32,
            )
            run_max[head] = new_max
            if first:
                run_sum[head] = weights
                mixed[head] = product
            else:
                shrink = jnp.exp2(old_max - new_max)
                run_sum[head] = run_sum[head] * shrink + weights
                mixed[head] = mixed[head] * shrink + product

    attend(0, 0, first=True)
    for h in (KEY, VAL):
        take(-3, 0, h)
        take(3, 0, h)
    attend(-1, 0)
    attend(1, 0)
    for h in (KEY, VAL):
        take(0, 1, h)
    attend(0, 1)
    attend(-2, 0)
    attend(2, 0)
    attend(-1, 1)
    attend(1, 1)
    for h in (KEY, VAL):
        take(-3, 1, h)
        take(3, 1, h)
    attend(-3, 0)
    attend(3, 0)
    for d, e in ((-2, 1), (2, 1), (4, 0)):
        for h in (KEY, VAL):
            take(d, e, h)
        attend(d, e)
    attend(-3, 1)
    attend(3, 1)
    for h in (KEY, VAL):
        take(4, 1, h)
    attend(4, 1)

    for head in range(heads):
        cols = slice(head * HEAD_DIM, (head + 1) * HEAD_DIM)
        total = jnp.sum(run_sum[head], axis=1, keepdims=True)
        attn[:, cols] = (mixed[head] / total).astype(jnp.bfloat16)

    loads[4].wait()
    for part in range(2):
        cols = slice(part * half, (part + 1) * half)
        partial[:, cols] = jnp.dot(
            attn[...], wo[:, cols], preferred_element_type=jnp.float32
        ).astype(jnp.bfloat16)
        for index, (dx, dy) in enumerate(peers):
            at = (((yl + dy) % 2) * NX + (x + dx) % NX) * rows
            back = peers.index(((-dx) % NX, dy))
            send(
                partial.at[pl.ds(pl.multiple_of(at, rows), rows), cols],
                parts.at[back, :, cols],
                sum_send.at[part, index],
                sum_recv.at[part, back],
                tensor_peer(dx, dy),
            )
    gate = token_mods(2)
    strength = jnp.zeros((rows, 128), jnp.float32)
    for r in range(8):
        strength = jnp.where(own_segs == r, strengths[r], strength)

    for part in range(2):
        cols = slice(part * half, (part + 1) * half)
        projected = partial[own_rows, cols].astype(jnp.float32)
        for index in range(len(peers)):
            arrived(parts.at[index, :, cols], sum_recv.at[part, index], sum_send.at[0, 0])
            projected = projected + parts[index, :, cols].astype(jnp.float32)
        branch[:, cols] = (
            hid[:, cols].astype(jnp.float32) + gate[:, cols] * projected
        ).astype(jnp.bfloat16)

    other_cols = pl.ds(pl.multiple_of((1 - cfg) * half, half), half)
    own_cols = pl.ds(pl.multiple_of(cfg * half, half), half)
    send(branch.at[:, other_cols], partner, pair_send, pair_recv, core)
    write = pltpu.make_async_copy(branch, branch_out, out_sem.at[0])
    write.start()
    arrived(partner, pair_recv, pair_send)
    mine = branch[:, own_cols].astype(jnp.float32)
    theirs = partner[...].astype(jnp.float32)
    first_branch = cfg == 0
    conditional = jnp.where(first_branch, mine, theirs)
    unconditional = jnp.where(first_branch, theirs, mine)
    wide = jnp.concatenate([strength] * (half // 128), axis=1)
    guided[...] = (unconditional + wide * (conditional - unconditional)).astype(jnp.bfloat16)
    last = pltpu.make_async_copy(guided, guided_out, out_sem.at[1])
    last.start()
    for copy in sent:
        copy.wait_send()
    write.wait()
    last.wait()


def body(hidden, stale_kv, w_qkv, w_out, mod_table, segment_ids, step_index, guide_scale):
    rows, width = hidden.shape[1:]
    slab = stale_kv.shape[2]
    local = w_qkv.shape[2]
    heads = local // HEAD_DIM
    bf16, f32 = jnp.bfloat16, jnp.float32
    anywhere = pl.BlockSpec(memory_space=pl.ANY)
    scalars = pl.BlockSpec(memory_space=pltpu.SMEM)
    dma = pltpu.SemaphoreType.DMA
    branch_rows, guided = pl.pallas_call(
        kernel,
        name="joint_attention",
        out_shape=(
            jax.ShapeDtypeStruct((rows, width), bf16),
            jax.ShapeDtypeStruct((rows, width // 2), bf16),
        ),
        in_specs=[anywhere] * 6 + [scalars] * 2,
        out_specs=(anywhere, anywhere),
        scratch_shapes=[
            pltpu.VMEM((rows, width), bf16),
            pltpu.VMEM((3, mod_table.shape[0], width), f32),
            pltpu.VMEM((NP, slab), jnp.int32),
            pltpu.VMEM((slab, slab), jnp.int32),
            pltpu.VMEM((3, width, local), bf16),
            pltpu.VMEM((local, width), bf16),
            pltpu.VMEM((slab, width), bf16),
            pltpu.VMEM((NP, 2, slab, local), bf16),
            pltpu.VMEM((slab, local), bf16),
            pltpu.VMEM((heads, slab, 128), f32),
            pltpu.VMEM((heads, slab, 128), f32),
            pltpu.VMEM((heads, slab, HEAD_DIM), f32),
            pltpu.VMEM((slab, local), bf16),
            pltpu.VMEM((slab, width), bf16),
            pltpu.VMEM((NT - 1, rows, width), bf16),
            pltpu.VMEM((rows, width), bf16),
            pltpu.VMEM((rows, width // 2), bf16),
            pltpu.VMEM((rows, width // 2), bf16),
            dma((5,)),
            dma((30,)),
            dma((NP, 2)),
            dma((7,)),
            dma((NT,)),
            dma((2, NT - 1)),
            dma((2, NT - 1)),
            dma,
            dma,
            dma((2,)),
        ],
        compiler_params=pltpu.CompilerParams(
            collective_id=0, has_side_effects=True, vmem_limit_bytes=62 << 20
        ),
    )(
        hidden[0],
        stale_kv[0],
        jnp.transpose(w_qkv, (1, 0, 2)),
        w_out,
        jnp.transpose(mod_table, (1, 0, 2)),
        segment_ids.reshape(NP, slab),
        step_index,
        guide_scale,
    )
    return branch_rows[None], guided


def solution(mesh):
    placed = (
        P("cfg", ("patch", "tensor"), None),
        P("cfg", None, "patch", "tensor"),
        P(None, None, "tensor"),
        P("tensor", None),
        P(),
        P(),
        P(),
        P(),
    )
    return jax.shard_map(
        body,
        mesh=mesh,
        in_specs=placed,
        out_specs=(P("cfg", ("patch", "tensor"), None), P(("patch", "tensor"), "cfg")),
        check_vma=False,
    )
```

time: 283 us -> 61.6 us (0.22)
  waiting for transfers between devices: 186 us -> 0 us
  Pallas kernels: 0 us -> 57.8 us
  local copies, waits for them, and re-layouts: 31.9 us -> 2.96 us
  blocking collectives: 25.4 us -> 0 us
  matrix products: 14.9 us -> 0 us
  between operations: 14 us -> 0.64 us
  starting transfers between devices: 5.84 us -> 0 us
  other arithmetic: 4.2 us -> 0 us
    all_gather x2 -> x0, waiting for transfers between devices: 108 us -> none  [the longest x1 74 us: body(): value_rows = lax.all_gather(stale_kv[0, 1], 'patch', axis=0, tiled=True)]
    psum x1 -> x0, waiting for transfers between devices: 76.3 us -> none  [body(): lax.psum(jnp.dot(attn, w_out, preferred_element_type=jnp.float32).astype(...]
    pallas_call x0 -> x1, Pallas kernels: none -> 57.8 us  [body(): pl.pallas_call(kernel, name='joint_attention', out_shape=(jax.ShapeDtypeS...]
    all_gather x1 -> x0, blocking collectives: 25.4 us -> none  [body(): lax.all_gather(modulated, 'tensor', axis=0, tiled=True)]
    dot_general x11 -> x0, matrix products: 14.9 us -> none  [the longest x1 5.36 us: body(): jnp.dot(lax.all_gather(modulated, 'tensor', axis=0, tiled=True), weights_...]
    reshape x4 -> x0, local copies, waits for them, and re-layouts: 11.6 us -> none  [the longest x1 5.12 us: body(): value_rows.reshape(block_count, block_rows, heads_here, HEAD_DIM)]
    unnamed x26 -> x2, local copies, waits for them, and re-layouts: 10.5 us -> 2.96 us
    while x9 -> x0, local copies, waits for them, and re-layouts: 6.08 us -> none  [the longest x3 6.07 us: body(): lax.scan(block_step, carry_state, (key_blocks, value_blocks, segment_bloc...]
  transfers between devices with their start and end apart: 4 -> 0, of which waited for: 4 -> 0; matrix products, arithmetic and copies ran while one was open for 11% -> 0% of each run, Pallas kernels for 0% -> 0%
where the time goes in v1:
time: 61.6 us; the launch traced here: 61.4 us
  Pallas kernels  57.8 us (94%)
  local copies, waits for them, and re-layouts  2.96 us (5%)
  between operations  0.64 us (1%)
    pallas_call x1, Pallas kernels, body(): pl.pallas_call(kernel, name='joint_attention', out_shape=(jax.ShapeDtypeS...  57.8 us
    unnamed x2, local copies, waits for them, and re-layouts  2.96 us

profile of v1, /device:TPU:1, one launch (start us, length us, event | category | flops | bytes accessed | tf_op | source)
XLA Modules:
  0.0 61.4 jit_solution(15353548462564316081)
XLA Ops:
  0.6 57.8 %joint_attention.1 = (bf16[16,3072]{1,0:T(8,128)(2,1)}, bf16[16,1536]{1,0:T(8,128)(2,1)}) custom-call(bf16[16,3072]{1,0:T(8,128)(2,1)} %bitcast.9, bf16[2,128,384]{2,1,0:T(8,128)(2,1)} %bitcast.8, bf16[3,3072,384]{2,1,0:T(8,128)(2,1)} %bitcast.6, bf16[384,3072]{1,0:T(8,128)(2,1)} %w_out.1, f32[3,32,3072]{2,1,0:T(8,128)} %bitcast.7, s32[16,128]{1,0:T(8,128)} %bitcast.11, ...), custom_call_target="tpu_custom_call" | custom-call | tf_op jit(solution)/shard_map/joint_attention/pallas_call | solution.py:360
  58.4 1.5 %copy.12 = bf16[1,16,3072]{2,1,0:T(8,128)(2,1)} copy(bf16[1,16,3072]{2,1,0:T(8,128)(2,1)} %bitcast.10) | data formatting | bytes 196608
  60.0 1.4 %copy.13 = bf16[16,1536]{1,0:T(8,128)(2,1)} copy(bf16[16,1536]{1,0:T(8,128)(2,1)} %get-tuple-element.9) | data formatting | bytes 98304

commit v2 on v1

v2 whole, which is shorter than its diff:
```python
import functools
import math

import jax
import jax.numpy as jnp
from jax import lax
from jax.experimental import pallas as pl
from jax.experimental.pallas import tpu as pltpu
from jax.sharding import PartitionSpec as P

MESH = pl.DeviceIdType.MESH
HEAD_DIM = 128
NZ = 8
NX = 4
NT = 8
NP = 16
KEY, VAL = 0, 1
NEG = -1e30


CHUNKS = 4
LANES = 128


def kernel(
    hidden,
    stale,
    w_qkv,
    w_out,
    mod_table,
    segments,
    step_index,
    guide_scale,
    branch,
    guided,
    hid,
    mods,
    segs,
    steps,
    strengths,
    query_segs,
    wq,
    wo,
    tokens,
    kv,
    fresh_kv,
    queries,
    far_queries,
    bias,
    scores,
    mixed,
    far_mixed,
    far_back,
    stats,
    stats_back,
    attn,
    partial,
    parts,
    partner,
    local_sem,
    kv_send,
    kv_recv,
    tok_send,
    tok_recv,
    far_send,
    far_recv,
    sum_send,
    sum_recv,
    pair_send,
    pair_recv,
):
    cfg = lax.axis_index("cfg")
    patch = lax.axis_index("patch")
    tensor = lax.axis_index("tensor")
    z, yh = patch // 2, patch % 2
    yl, x = tensor // NX, tensor % NX
    rows, width = hid.shape
    half = width // 2
    slab = queries.shape[0]
    heads = queries.shape[1] // HEAD_DIM
    chunk = 2 * slab // CHUNKS

    def tensor_peer(dx, dy):
        return (cfg, patch, ((yl + dy) % 2) * NX + (x + dx) % NX)

    up = (cfg, ((z + 1) % NZ) * 2 + yh, tensor)
    down = (cfg, ((z + NZ - 1) % NZ) * 2 + yh, tensor)
    across = (cfg, z * 2 + (1 - yh), tensor)
    core = (1 - cfg, patch, tensor)
    peers = [(dx, dy) for dy in (0, 1) for dx in range(NX) if (dx, dy) != (0, 0)]

    loads = [
        pltpu.make_async_copy(hidden, hid, local_sem.at[0]),
        pltpu.make_async_copy(segments, segs, local_sem.at[1]),
        pltpu.make_async_copy(step_index, steps, local_sem.at[6]),
        pltpu.make_async_copy(guide_scale, strengths, local_sem.at[7]),
        pltpu.make_async_copy(mod_table, mods, local_sem.at[2]),
        pltpu.make_async_copy(w_qkv, wq, local_sem.at[3]),
        pltpu.make_async_copy(w_out, wo, local_sem.at[4]),
        pltpu.make_async_copy(stale, kv.at[0], local_sem.at[5]),
    ]
    for load in loads[:5]:
        load.start()

    barrier = pltpu.get_barrier_semaphore()
    greeted = [up, down, across, core] + [tensor_peer(dx, dy) for dx, dy in peers]
    for device in greeted:
        pl.semaphore_signal(barrier, inc=1, device_id=device, device_id_type=MESH)

    sent = []

    def send(src, dst, send_sem, recv_sem, device):
        copy = pltpu.make_async_remote_copy(
            src_ref=src,
            dst_ref=dst,
            send_sem=send_sem,
            recv_sem=recv_sem,
            device_id=device,
            device_id_type=MESH,
        )
        copy.start()
        sent.append(copy)

    def arrived(dst, recv_sem, send_sem):
        pltpu.make_async_remote_copy(
            src_ref=dst,
            dst_ref=dst,
            send_sem=send_sem,
            recv_sem=recv_sem,
            device_id=core,
            device_id_type=MESH,
        ).wait_recv()

    counter = [0]

    def block_of(ref, c):
        return ref.at[c // (CHUNKS // 2), pl.ds(c % (CHUNKS // 2) * chunk, chunk), :]

    def send_kv(src, d, c, device):
        send(
            src,
            block_of(kv.at[d % NZ], c),
            kv_send.at[counter[0]],
            kv_recv.at[d % NZ, c],
            device,
        )
        counter[0] += 1

    def take(d, c):
        here = block_of(kv.at[d % NZ], c)
        arrived(here, kv_recv.at[d % NZ, c], kv_send.at[0])
        if -3 < d < 0 or (d == -3 and c < CHUNKS // 2):
            send_kv(here, d - 1, c, up)
        if 0 < d < 3 or (d == 3 and c >= CHUNKS // 2):
            send_kv(here, d + 1, c, down)

    def token_rows(dx, dy):
        at = (((yl + dy) % 2) * NX + (x + dx) % NX) * rows
        return tokens.at[pl.ds(pl.multiple_of(at, rows), rows), :]

    def send_tokens(dy, dx_to, index):
        block = token_rows(0, dy)
        slot = dy * NX + (-dx_to) % NX
        send(block, block, tok_send.at[index], tok_recv.at[slot], tensor_peer(dx_to, 0))

    def wait_tokens(dx, dy):
        arrived(token_rows(dx, dy), tok_recv.at[dy * NX + dx], tok_send.at[0])

    loads[0].wait()
    residual = hid[...].astype(jnp.float32)
    mean = jnp.sum(residual, axis=-1, keepdims=True) * (1.0 / width)
    centred = residual - mean
    var = jnp.sum(centred * centred, axis=-1, keepdims=True) * (1.0 / width)
    normed = centred * lax.rsqrt(var + 1e-6)

    pl.semaphore_wait(barrier, len(greeted))
    for c in range(CHUNKS):
        send_kv(block_of(stale, c), -1, c, up)
        send_kv(block_of(stale, c), 1, c, down)

    def column(which):
        row = segs[pl.ds(which, 1), :]
        return jnp.broadcast_to(row, (slab, slab)).T

    loads[1].wait()
    query_segs[...] = column(patch)
    own_segs = query_segs[pl.ds(pl.multiple_of(tensor * rows, rows), rows), :]
    for load in loads[2:5]:
        load.wait()

    def token_mods(which):
        wide = jnp.concatenate([own_segs] * (width // LANES), axis=1)
        picked = jnp.zeros((rows, width), jnp.float32)
        for r in range(8):
            row = mods[which, pl.ds(steps[r], 1), :]
            picked = jnp.where(wide == r, row, picked)
        return picked

    own_rows = pl.ds(pl.multiple_of(tensor * rows, rows), rows)
    tokens[own_rows, :] = (normed * (1.0 + token_mods(1)) + token_mods(0)).astype(jnp.bfloat16)

    block = token_rows(0, 0)
    send(block, block, tok_send.at[0], tok_recv.at[NX], tensor_peer(0, 1))
    for index, dx in enumerate((1, NX - 1, 2)):
        send_tokens(0, dx, 1 + index)
    for load in loads[5:]:
        load.start()

    def fill_bias(which, seg_column):
        for d in range(NZ):
            key_row = segs[pl.ds(((z + d) % NZ) * 2 + yh, 1), :]
            bias[which, :, d * slab : (d + 1) * slab] = jnp.where(seg_column == key_row, 0.0, NEG)

    wait_tokens(0, 1)
    for index, dx in enumerate((1, NX - 1, 2)):
        send_tokens(1, dx, 4 + index)
    for c in range(CHUNKS):
        take(-1, c)
        take(1, c)
    fill_bias(0, query_segs[...])
    fill_bias(1, column(z * 2 + (1 - yh)))
    for c in range(CHUNKS):
        take(-2, c)
        take(2, c)
    for dx, dy in peers:
        if (dx, dy) != (0, 1):
            wait_tokens(dx, dy)
    loads[5].wait()
    queries[...] = jnp.dot(tokens[...], wq[0], preferred_element_type=jnp.float32).astype(
        jnp.bfloat16
    )
    send(queries, far_queries, far_send.at[0], far_recv.at[0], across)
    for c in range(CHUNKS):
        take(-3, c)
        take(3, c)
    for j in (KEY, VAL):
        fresh_kv[j] = jnp.dot(
            tokens[...], wq[1 + j], preferred_element_type=jnp.float32
        ).astype(jnp.bfloat16)

    scale = math.log2(math.e) / HEAD_DIM**0.5
    step = 2
    span = step * slab

    def score(which, q_ref, head):
        cols = slice(head * HEAD_DIM, (head + 1) * HEAD_DIM)
        top = None
        for i in range(NZ // step):
            keys = kv[i * step : (i + 1) * step, KEY, :, cols].reshape(span, HEAD_DIM)
            found = lax.dot_general(
                q_ref[:, cols], keys, (((1,), (1,)), ((), ())), preferred_element_type=jnp.float32
            )
            at = slice(i * span, (i + 1) * span)
            found = found * scale + bias[which, :, at]
            scores[head, :, at] = found
            for k in range(step):
                piece = found[:, k * slab : (k + 1) * slab]
                top = piece if top is None else jnp.maximum(top, piece)
        return jnp.max(top, axis=1, keepdims=True)

    def mix(head, top):
        cols = slice(head * HEAD_DIM, (head + 1) * HEAD_DIM)
        total, result = None, None
        for i in range(NZ // step):
            weights = jnp.exp2(scores[head, :, i * span : (i + 1) * span] - top)
            values = kv[i * step : (i + 1) * step, VAL, :, cols].reshape(span, HEAD_DIM)
            product = jnp.dot(
                weights.astype(jnp.bfloat16), values, preferred_element_type=jnp.float32
            )
            result = product if result is None else result + product
            for k in range(step):
                piece = weights[:, k * slab : (k + 1) * slab]
                total = piece if total is None else total + piece
        return jnp.sum(total, axis=1, keepdims=True), result

    arrived(far_queries, far_recv.at[0], far_send.at[0])
    loads[7].wait()
    for c in range(CHUNKS):
        take(4, c)
    lane = lax.broadcasted_iota(jnp.int32, (slab, LANES), 1)
    packed = jnp.zeros((slab, LANES), jnp.float32)
    tops = [score(1, far_queries, head) for head in range(heads)]
    for head in range(heads):
        total, result = mix(head, tops[head])
        far_mixed[head] = result.astype(jnp.bfloat16)
        send(
            far_mixed.at[head],
            far_back.at[head],
            far_send.at[1 + head],
            far_recv.at[1 + head],
            across,
        )
        packed = jnp.where(lane == head, tops[head], packed)
        packed = jnp.where(lane == heads + head, total, packed)
    stats[...] = packed.T[:8]
    send(stats, stats_back, far_send.at[1 + heads], far_recv.at[1 + heads], across)

    for j in (KEY, VAL):
        kv[0, j] = fresh_kv[j]
    tops = [score(0, queries, head) for head in range(heads)]
    own = [mix(head, tops[head]) for head in range(heads)]
    for head in range(heads):
        mixed[head] = own[head][1]

    arrived(stats_back, far_recv.at[1 + heads], far_send.at[0])
    back = jnp.concatenate([stats_back[...]] * (LANES // 8), axis=0).T
    for head in range(heads):
        cols = slice(head * HEAD_DIM, (head + 1) * HEAD_DIM)
        far_top, far_total = back[:, head : head + 1], back[:, heads + head : heads + head + 1]
        top = jnp.maximum(tops[head], far_top)
        near_part, far_part = jnp.exp2(tops[head] - top), jnp.exp2(far_top - top)
        total = own[head][0] * near_part + far_total * far_part
        arrived(far_back.at[head], far_recv.at[1 + head], far_send.at[0])
        result = mixed[head] * near_part + far_back[head].astype(jnp.float32) * far_part
        attn[:, cols] = (result / total).astype(jnp.bfloat16)

    loads[6].wait()
    for part in range(2):
        cols = slice(part * half, (part + 1) * half)
        partial[:, cols] = jnp.dot(
            attn[...], wo[:, cols], preferred_element_type=jnp.float32
        ).astype(jnp.bfloat16)
        for index, (dx, dy) in enumerate(peers):
            at = (((yl + dy) % 2) * NX + (x + dx) % NX) * rows
            slot = peers.index(((-dx) % NX, dy))
            send(
                partial.at[pl.ds(pl.multiple_of(at, rows), rows), cols],
                parts.at[slot, :, cols],
                sum_send.at[part, index],
                sum_recv.at[part, slot],
                tensor_peer(dx, dy),
            )
    gate = token_mods(2)
    strength = jnp.zeros((rows, LANES), jnp.float32)
    for r in range(8):
        strength = jnp.where(own_segs == r, strengths[r], strength)

    for part in range(2):
        cols = slice(part * half, (part + 1) * half)
        projected = partial[own_rows, cols].astype(jnp.float32)
        for index in range(len(peers)):
            arrived(parts.at[index, :, cols], sum_recv.at[part, index], sum_send.at[0, 0])
            projected = projected + parts[index, :, cols].astype(jnp.float32)
        branch[:, cols] = (
            hid[:, cols].astype(jnp.float32) + gate[:, cols] * projected
        ).astype(jnp.bfloat16)

    other_cols = pl.ds(pl.multiple_of((1 - cfg) * half, half), half)
    own_cols = pl.ds(pl.multiple_of(cfg * half, half), half)
    send(branch.at[:, other_cols], partner, pair_send, pair_recv, core)
    arrived(partner, pair_recv, pair_send)
    mine = branch[:, own_cols].astype(jnp.float32)
    theirs = partner[...].astype(jnp.float32)
    first_branch = cfg == 0
    conditional = jnp.where(first_branch, mine, theirs)
    unconditional = jnp.where(first_branch, theirs, mine)
    wide = jnp.concatenate([strength] * (half // LANES), axis=1)
    guided[...] = (unconditional + wide * (conditional - unconditional)).astype(jnp.bfloat16)
    for copy in sent:
        copy.wait_send()


def body(hidden, stale_kv, w_qkv, w_out, mod_table, segment_ids, step_index, guide_scale):
    rows, width = hidden.shape[1:]
    slab = stale_kv.shape[2]
    local = w_qkv.shape[2]
    heads = local // HEAD_DIM
    bf16, f32 = jnp.bfloat16, jnp.float32
    anywhere = pl.BlockSpec(memory_space=pl.ANY)
    dma = pltpu.SemaphoreType.DMA
    def pinned(array):
        return pltpu.with_memory_space_constraint(array, pltpu.HBM)

    branch_rows, guided = pl.pallas_call(
        kernel,
        name="joint_attention",
        out_shape=(
            pltpu.VMEM((rows, width), bf16),
            pltpu.VMEM((rows, width // 2), bf16),
        ),
        in_specs=[anywhere] * 8,
        out_specs=(
            pl.BlockSpec(memory_space=pltpu.VMEM),
            pl.BlockSpec(memory_space=pltpu.VMEM),
        ),
        scratch_shapes=[
            pltpu.VMEM((rows, width), bf16),
            pltpu.VMEM((3, mod_table.shape[0], width), f32),
            pltpu.VMEM((NP, slab), jnp.int32),
            pltpu.SMEM(step_index.shape, jnp.int32),
            pltpu.SMEM(guide_scale.shape, f32),
            pltpu.VMEM((slab, slab), jnp.int32),
            pltpu.VMEM((3, width, local), bf16),
            pltpu.VMEM((local, width), bf16),
            pltpu.VMEM((slab, width), bf16),
            pltpu.VMEM((NZ, 2, slab, local), bf16),
            pltpu.VMEM((2, slab, local), bf16),
            pltpu.VMEM((slab, local), bf16),
            pltpu.VMEM((slab, local), bf16),
            pltpu.VMEM((2, slab, NZ * slab), f32),
            pltpu.VMEM((heads, slab, NZ * slab), f32),
            pltpu.VMEM((heads, slab, HEAD_DIM), f32),
            pltpu.VMEM((heads, slab, HEAD_DIM), bf16),
            pltpu.VMEM((heads, slab, HEAD_DIM), bf16),
            pltpu.VMEM((8, LANES), f32),
            pltpu.VMEM((8, LANES), f32),
            pltpu.VMEM((slab, local), bf16),
            pltpu.VMEM((slab, width), bf16),
            pltpu.VMEM((NT - 1, rows, width), bf16),
            pltpu.VMEM((rows, width // 2), bf16),
            dma((8,)),
            dma((7 * CHUNKS,)),
            dma((NZ, CHUNKS)),
            dma((7,)),
            dma((NT,)),
            dma((2 + heads,)),
            dma((2 + heads,)),
            dma((2, NT - 1)),
            dma((2, NT - 1)),
            dma,
            dma,
        ],
        compiler_params=pltpu.CompilerParams(
            collective_id=0, has_side_effects=True, vmem_limit_bytes=48 << 20
        ),
    )(
        pinned(hidden[0]),
        pinned(stale_kv[0]),
        pinned(jnp.transpose(w_qkv, (1, 0, 2))),
        pinned(w_out),
        pinned(jnp.transpose(mod_table, (1, 0, 2))),
        pinned(segment_ids.reshape(NP, slab)),
        pinned(step_index),
        pinned(guide_scale),
    )
    return branch_rows[None], guided


def solution(mesh):
    placed = (
        P("cfg", ("patch", "tensor"), None),
        P("cfg", None, "patch", "tensor"),
        P(None, None, "tensor"),
        P("tensor", None),
        P(),
        P(),
        P(),
        P(),
    )
    return jax.shard_map(
        body,
        mesh=mesh,
        in_specs=placed,
        out_specs=(P("cfg", ("patch", "tensor"), None), P(("patch", "tensor"), "cfg")),
        check_vma=False,
    )
```

time: 61.6 us -> 46.9 us (0.76)
  Pallas kernels: 57.8 us -> 44.9 us
  local copies, waits for them, and re-layouts: 2.96 us -> 1.26 us
    pallas_call x1, Pallas kernels: 57.8 us -> 44.9 us  [body(): pl.pallas_call(kernel, name='joint_attention', out_shape=(pltpu.VMEM((row...]
    unnamed x2, local copies, waits for them, and re-layouts: 2.96 us -> 1.26 us
where the time goes in v2:
time: 46.9 us; the launch traced here: 46.8 us
  Pallas kernels  44.9 us (96%)
  local copies, waits for them, and re-layouts  1.26 us (3%)
  between operations  0.64 us (1%)
    pallas_call x1, Pallas kernels, body(): pl.pallas_call(kernel, name='joint_attention', out_shape=(pltpu.VMEM((row...  44.9 us
    unnamed x2, local copies, waits for them, and re-layouts  1.26 us

profile of v2, /device:TPU:1, one launch (start us, length us, event | category | flops | bytes accessed | tf_op | source)
XLA Modules:
  0.0 46.8 jit_solution(12144996826157764903)
XLA Ops:
  0.6 44.9 %joint_attention.1 = (bf16[16,3072]{1,0:T(8,128)(2,1)S(1)}, bf16[16,1536]{1,0:T(8,128)(2,1)S(1)}) custom-call(bf16[16,3072]{1,0:T(8,128)(2,1)} %bitcast.10, bf16[2,128,384]{2,1,0:T(8,128)(2,1)} %bitcast.9, bf16[3,3072,384]{2,1,0:T(8,128)(2,1)} %bitcast.7, bf16[384,3072]{1,0:T(8,128)(2,1)} %w_out.1, f32[3,32,3072]{2,1,0:T(8,128)} %bitcast.8, ...), custom_call_target="tpu_custom_call" | custom-call | tf_op jit(solution)/shard_map/joint_attention/pallas_call | solution.py:374
  45.5 0.6 %copy.12 = bf16[1,16,3072]{2,1,0:T(8,128)(2,1)} copy(bf16[1,16,3072]{2,1,0:T(8,128)(2,1)S(1)} %bitcast.6) | data formatting | bytes 196608
  46.2 0.6 %copy.13 = bf16[16,1536]{1,0:T(8,128)(2,1)} copy(bf16[16,1536]{1,0:T(8,128)(2,1)S(1)} %get-tuple-element.7) | data formatting | bytes 98304

commit v3 on v2

v3 whole, which is shorter than its diff:
```python
import functools
import math

import jax
import jax.numpy as jnp
from jax import lax
from jax.experimental import pallas as pl
from jax.experimental.pallas import tpu as pltpu
from jax.sharding import PartitionSpec as P

MESH = pl.DeviceIdType.MESH
HEAD_DIM = 128
NZ = 8
NX = 4
NT = 8
NP = 16
KEY, VAL = 0, 1
NEG = -1e30


PARTS = 1
CHUNKS = 4
LANES = 128


def kernel(
    hidden,
    stale,
    w_qkv,
    w_out,
    mod_table,
    segments,
    step_index,
    guide_scale,
    branch,
    guided,
    hid,
    mods,
    segs,
    steps,
    strengths,
    query_segs,
    wq,
    wo,
    tokens,
    kv,
    fresh_kv,
    queries,
    far_queries,
    bias,
    scores,
    far_mixed,
    far_back,
    stats,
    stats_back,
    attn,
    partial,
    hops,
    onward,
    parts,
    partner,
    local_sem,
    kv_send,
    kv_recv,
    tok_send,
    tok_recv,
    far_send,
    far_recv,
    sum_send,
    sum_recv,
    pair_send,
    pair_recv,
):
    cfg = lax.axis_index("cfg")
    patch = lax.axis_index("patch")
    tensor = lax.axis_index("tensor")
    z, yh = patch // 2, patch % 2
    yl, x = tensor // NX, tensor % NX
    rows, width = hid.shape
    half = width // 2
    slab = queries.shape[0]
    heads = queries.shape[1] // HEAD_DIM
    chunk = 2 * slab // CHUNKS

    def tensor_peer(dx, dy):
        return (cfg, patch, ((yl + dy) % 2) * NX + (x + dx) % NX)

    up = (cfg, ((z + 1) % NZ) * 2 + yh, tensor)
    down = (cfg, ((z + NZ - 1) % NZ) * 2 + yh, tensor)
    across = (cfg, z * 2 + (1 - yh), tensor)
    core = (1 - cfg, patch, tensor)

    barrier = pltpu.get_barrier_semaphore()
    greeted = [up, down, across, core] + [tensor_peer(*to) for to in ((1, 0), (NX - 1, 0), (2, 0), (0, 1))]
    for device in greeted:
        pl.semaphore_signal(barrier, inc=1, device_id=device, device_id_type=MESH)

    loads = [
        pltpu.make_async_copy(hidden, hid, local_sem.at[0]),
        pltpu.make_async_copy(segments, segs, local_sem.at[1]),
        pltpu.make_async_copy(step_index, steps, local_sem.at[6]),
        pltpu.make_async_copy(guide_scale, strengths, local_sem.at[7]),
        pltpu.make_async_copy(mod_table, mods, local_sem.at[2]),
        pltpu.make_async_copy(w_qkv, wq, local_sem.at[3]),
        pltpu.make_async_copy(w_out, wo, local_sem.at[4]),
        pltpu.make_async_copy(stale, kv.at[0], local_sem.at[5]),
    ]
    for load in loads[:5]:
        load.start()

    sent = []

    def send(src, dst, send_sem, recv_sem, device):
        copy = pltpu.make_async_remote_copy(
            src_ref=src,
            dst_ref=dst,
            send_sem=send_sem,
            recv_sem=recv_sem,
            device_id=device,
            device_id_type=MESH,
        )
        copy.start()
        sent.append(copy)

    def arrived(dst, recv_sem, send_sem):
        pltpu.make_async_remote_copy(
            src_ref=dst,
            dst_ref=dst,
            send_sem=send_sem,
            recv_sem=recv_sem,
            device_id=core,
            device_id_type=MESH,
        ).wait_recv()

    counter = [0]

    def swap(c):
        return (c + CHUNKS // 2) % CHUNKS

    def block_of(ref, c):
        return ref.at[c // (CHUNKS // 2), pl.ds(c % (CHUNKS // 2) * chunk, chunk), :]

    def send_kv(src, d, c, device):
        send(
            src,
            block_of(kv.at[d % NZ], c),
            kv_send.at[counter[0]],
            kv_recv.at[d % NZ, c],
            device,
        )
        counter[0] += 1

    def take(d, c):
        here = block_of(kv.at[d % NZ], c)
        arrived(here, kv_recv.at[d % NZ, c], kv_send.at[0])
        if -3 < d < 0 or (d == -3 and c < CHUNKS // 2):
            send_kv(here, d - 1, c, up)
        if 0 < d < 3 or (d == 3 and c >= CHUNKS // 2):
            send_kv(here, d + 1, c, down)

    def token_block(dx, dy, part):
        at = (((yl + dy) % 2) * NX + (x + dx) % NX) * rows
        return tokens.at[pl.ds(pl.multiple_of(at, rows), rows), part * half : (part + 1) * half]

    def send_tokens(dx, dy, to_dx, to_dy, index, part):
        block = token_block(dx, dy, part)
        slot = ((dy + to_dy) % 2) * NX + (dx - to_dx) % NX
        send(
            block,
            block,
            tok_send.at[part, index],
            tok_recv.at[part, slot],
            tensor_peer(to_dx, to_dy),
        )

    def wait_tokens(dx, dy, part):
        arrived(token_block(dx, dy, part), tok_recv.at[part, dy * NX + dx], tok_send.at[0, 0])

    def relay_tokens(part):
        for index, dx in enumerate((1, NX - 1)):
            wait_tokens(dx, 0, part)
            send_tokens(dx, 0, 0, 1, 4 + index, part)
        wait_tokens(0, 1, part)
        send_tokens(0, 1, 2, 0, 6, part)

    pl.semaphore_wait(barrier, len(greeted))
    for c in range(CHUNKS):
        send_kv(block_of(stale, c), -1, c, up)
        send_kv(block_of(stale, swap(c)), 1, swap(c), down)

    loads[0].wait()
    residual = hid[...].astype(jnp.float32)
    mean = jnp.sum(residual, axis=-1, keepdims=True) * (1.0 / width)
    centred = residual - mean
    var = jnp.sum(centred * centred, axis=-1, keepdims=True) * (1.0 / width)
    normed = centred * lax.rsqrt(var + 1e-6)

    def column(which):
        row = segs[pl.ds(which, 1), :]
        return jnp.broadcast_to(row, (slab, slab)).T

    loads[1].wait()
    query_segs[...] = column(patch)
    own_segs = query_segs[pl.ds(pl.multiple_of(tensor * rows, rows), rows), :]
    for load in loads[2:5]:
        load.wait()

    def token_mods(which, start, count):
        wide = jnp.concatenate([own_segs] * (count // LANES), axis=1)
        picked = jnp.zeros((rows, count), jnp.float32)
        for r in range(8):
            row = mods[which, pl.ds(steps[r], 1), pl.ds(start, count)]
            picked = jnp.where(wide == r, row, picked)
        return picked

    own_rows = pl.ds(pl.multiple_of(tensor * rows, rows), rows)
    shift, scale = token_mods(0, 0, width), token_mods(1, 0, width)
    tokens[own_rows, :] = (normed * (1.0 + scale) + shift).astype(jnp.bfloat16)

    for part in range(2):
        send_tokens(0, 0, 1, 0, 0, part)
        send_tokens(0, 0, NX - 1, 0, 1, part)
        send_tokens(0, 0, 0, 1, 2, part)
    for part in range(2):
        send_tokens(0, 0, 2, 0, 3, part)
    for load in loads[5:]:
        load.start()

    def fill_bias(which, seg_column):
        for d in range(NZ):
            key_row = segs[pl.ds(((z + d) % NZ) * 2 + yh, 1), :]
            bias[which, :, d * slab : (d + 1) * slab] = jnp.where(seg_column == key_row, 0.0, NEG)

    def take_both(d, c):
        take(-d, c)
        take(d, swap(c))

    for part in range(2):
        relay_tokens(part)
        for c in range(part * CHUNKS // 2, (part + 1) * CHUNKS // 2):
            take_both(1, c)
    fill_bias(0, query_segs[...])
    fill_bias(1, column(z * 2 + (1 - yh)))
    for c in range(CHUNKS):
        take_both(2, c)
    for part in range(2):
        for dx, dy in ((2, 0), (1, 1), (NX - 1, 1), (2, 1)):
            wait_tokens(dx, dy, part)
    loads[5].wait()
    queries[...] = jnp.dot(tokens[...], wq[0], preferred_element_type=jnp.float32).astype(
        jnp.bfloat16
    )
    send(queries, far_queries, far_send.at[0], far_recv.at[0], across)
    for c in range(CHUNKS):
        take_both(3, c)
    for j in (KEY, VAL):
        fresh_kv[j] = jnp.dot(
            tokens[...], wq[1 + j], preferred_element_type=jnp.float32
        ).astype(jnp.bfloat16)

    scale = math.log2(math.e) / HEAD_DIM**0.5

    def meet(which, q_ref, runs):
        cols = [slice(head * HEAD_DIM, (head + 1) * HEAD_DIM) for head in range(heads)]
        tops = []
        for head in range(heads):
            top = None
            for first, count in runs:
                at = slice(first * slab, (first + count) * slab)
                keys = kv[first : first + count, KEY, :, cols[head]].reshape(count * slab, HEAD_DIM)
                found = lax.dot_general(
                    q_ref[:, cols[head]],
                    keys,
                    (((1,), (1,)), ((), ())),
                    preferred_element_type=jnp.float32,
                )
                found = found * scale + bias[which, :, at]
                scores[head, :, at] = found
                for k in range(count):
                    piece = found[:, k * slab : (k + 1) * slab]
                    top = piece if top is None else jnp.maximum(top, piece)
            tops.append(jnp.max(top, axis=1, keepdims=True))
        met = []
        for head in range(heads):
            total, result = None, None
            for first, count in runs:
                at = slice(first * slab, (first + count) * slab)
                weights = jnp.exp2(scores[head, :, at] - tops[head])
                values = kv[first : first + count, VAL, :, cols[head]].reshape(
                    count * slab, HEAD_DIM
                )
                product = jnp.dot(
                    weights.astype(jnp.bfloat16), values, preferred_element_type=jnp.float32
                )
                result = product if result is None else result + product
                for k in range(count):
                    piece = weights[:, k * slab : (k + 1) * slab]
                    total = piece if total is None else total + piece
            met.append((tops[head], jnp.sum(total, axis=1, keepdims=True), result))
        return met

    def merge(one, two):
        top = jnp.maximum(one[0], two[0])
        left, right = jnp.exp2(one[0] - top), jnp.exp2(two[0] - top)
        return top, one[1] * left + two[1] * right, one[2] * left + two[2] * right

    early, late = ((0, 2), (2, 2), (5, 3)), ((4, 1),)

    arrived(far_queries, far_recv.at[0], far_send.at[0])
    loads[7].wait()
    far = meet(1, far_queries, early)
    for j in (KEY, VAL):
        kv[0, j] = fresh_kv[j]
    own = meet(0, queries, early)
    for c in range(CHUNKS // 2):
        take(4, c)
        take(4, swap(c))
    lane = lax.broadcasted_iota(jnp.int32, (slab, LANES), 1)
    packed = jnp.zeros((slab, LANES), jnp.float32)
    far_late = meet(1, far_queries, late)
    for head in range(heads):
        top, total, result = merge(far[head], far_late[head])
        far_mixed[head] = result.astype(jnp.bfloat16)
        send(
            far_mixed.at[head],
            far_back.at[head],
            far_send.at[1 + head],
            far_recv.at[1 + head],
            across,
        )
        packed = jnp.where(lane == head, top, packed)
        packed = jnp.where(lane == heads + head, total, packed)
    stats[...] = packed.T[:8]
    send(stats, stats_back, far_send.at[1 + heads], far_recv.at[1 + heads], across)
    own_late = meet(0, queries, late)
    own = [merge(own[head], own_late[head]) for head in range(heads)]

    arrived(stats_back, far_recv.at[1 + heads], far_send.at[0])
    back = jnp.concatenate([stats_back[...]] * (LANES // 8), axis=0).T
    for head in range(heads):
        cols = slice(head * HEAD_DIM, (head + 1) * HEAD_DIM)
        arrived(far_back.at[head], far_recv.at[1 + head], far_send.at[0])
        top, total, result = merge(
            own[head],
            (
                back[:, head : head + 1],
                back[:, heads + head : heads + head + 1],
                far_back[head].astype(jnp.float32),
            ),
        )
        attn[:, cols] = (result / total).astype(jnp.bfloat16)

    piece = half // PARTS
    starts = [
        pl.multiple_of(which * half + part * piece, piece)
        for which in (1 - cfg, cfg)
        for part in range(PARTS)
    ]
    loads[6].wait()

    def sum_rows(dx, dy):
        at = (((yl + dy) % 2) * NX + (x + dx) % NX) * rows
        return pl.ds(pl.multiple_of(at, rows), rows)

    for part in range(2 * PARTS):
        partial[part] = jnp.dot(
            attn[...], wo[:, pl.ds(starts[part], piece)], preferred_element_type=jnp.float32
        ).astype(jnp.bfloat16)
        for index, (row, to, landing) in enumerate(
            (
                (sum_rows(1, 1), tensor_peer(0, 1), hops.at[part, 0]),
                (sum_rows(NX - 1, 1), tensor_peer(0, 1), hops.at[part, 1]),
                (sum_rows(2, 1), tensor_peer(2, 0), hops.at[part, 2]),
                (sum_rows(2, 0), tensor_peer(2, 0), parts.at[part, 2]),
            )
        ):
            send(
                partial.at[part, row, :],
                landing,
                sum_send.at[part, index],
                sum_recv.at[part, index],
                to,
            )
    strength = jnp.zeros((rows, LANES), jnp.float32)
    for r in range(8):
        strength = jnp.where(own_segs == r, strengths[r], strength)
    gates = [token_mods(2, start, piece) for start in starts]

    for part in range(2 * PARTS):
        for index, (row, to, slot) in enumerate(
            (
                (sum_rows(1, 0), tensor_peer(1, 0), 0),
                (sum_rows(NX - 1, 0), tensor_peer(NX - 1, 0), 1),
                (sum_rows(0, 1), tensor_peer(0, 1), 3),
            )
        ):
            arrived(hops.at[part, index], sum_recv.at[part, index], sum_send.at[0, 0])
            both = hops[part, index].astype(jnp.float32) + partial[part, row, :].astype(jnp.float32)
            onward[part, index] = both.astype(jnp.bfloat16)
            send(
                onward.at[part, index],
                parts.at[part, slot],
                sum_send.at[part, 4 + index],
                sum_recv.at[part, 4 + index],
                to,
            )

    sums = []
    for part in range(2 * PARTS):
        cols = pl.ds(starts[part], piece)
        projected = partial[part, own_rows, :].astype(jnp.float32)
        for slot, sem in ((2, 3), (0, 4), (1, 5), (3, 6)):
            arrived(parts.at[part, slot], sum_recv.at[part, sem], sum_send.at[0, 0])
            projected = projected + parts[part, slot].astype(jnp.float32)
        total = hid[:, cols].astype(jnp.float32) + gates[part] * projected
        sums.append(total.astype(jnp.bfloat16))
        branch[:, cols] = sums[part]
        if part < PARTS:
            send(branch.at[:, cols], partner.at[part], pair_send.at[part], pair_recv.at[part], core)

    first_branch = cfg == 0
    wide = jnp.concatenate([strength] * (piece // LANES), axis=1)
    for part in range(PARTS):
        arrived(partner.at[part], pair_recv.at[part], pair_send.at[0])
        mine = sums[PARTS + part].astype(jnp.float32)
        theirs = partner[part].astype(jnp.float32)
        conditional = jnp.where(first_branch, mine, theirs)
        unconditional = jnp.where(first_branch, theirs, mine)
        guided[:, part * piece : (part + 1) * piece] = (
            unconditional + wide * (conditional - unconditional)
        ).astype(jnp.bfloat16)
    for copy in sent:
        copy.wait_send()


def body(hidden, stale_kv, w_qkv, w_out, mod_table, segment_ids, step_index, guide_scale):
    rows, width = hidden.shape[1:]
    slab = stale_kv.shape[2]
    local = w_qkv.shape[2]
    heads = local // HEAD_DIM
    piece = width // 2 // PARTS
    bf16, f32 = jnp.bfloat16, jnp.float32
    anywhere = pl.BlockSpec(memory_space=pl.ANY)
    dma = pltpu.SemaphoreType.DMA
    def pinned(array):
        return pltpu.with_memory_space_constraint(array, pltpu.HBM)

    branch_rows, guided = pl.pallas_call(
        kernel,
        name="joint_attention",
        out_shape=(
            pltpu.VMEM((rows, width), bf16),
            pltpu.VMEM((rows, width // 2), bf16),
        ),
        in_specs=[anywhere] * 8,
        out_specs=(
            pl.BlockSpec(memory_space=pltpu.VMEM),
            pl.BlockSpec(memory_space=pltpu.VMEM),
        ),
        scratch_shapes=[
            pltpu.VMEM((rows, width), bf16),
            pltpu.VMEM((3, mod_table.shape[0], width), f32),
            pltpu.VMEM((NP, slab), jnp.int32),
            pltpu.SMEM(step_index.shape, jnp.int32),
            pltpu.SMEM(guide_scale.shape, f32),
            pltpu.VMEM((slab, slab), jnp.int32),
            pltpu.VMEM((3, width, local), bf16),
            pltpu.VMEM((local, width), bf16),
            pltpu.VMEM((slab, width), bf16),
            pltpu.VMEM((NZ, 2, slab, local), bf16),
            pltpu.VMEM((2, slab, local), bf16),
            pltpu.VMEM((slab, local), bf16),
            pltpu.VMEM((slab, local), bf16),
            pltpu.VMEM((2, slab, NZ * slab), f32),
            pltpu.VMEM((heads, slab, NZ * slab), f32),
            pltpu.VMEM((heads, slab, HEAD_DIM), bf16),
            pltpu.VMEM((heads, slab, HEAD_DIM), bf16),
            pltpu.VMEM((8, LANES), f32),
            pltpu.VMEM((8, LANES), f32),
            pltpu.VMEM((slab, local), bf16),
            pltpu.VMEM((2 * PARTS, slab, piece), bf16),
            pltpu.VMEM((2 * PARTS, 3, rows, piece), bf16),
            pltpu.VMEM((2 * PARTS, 3, rows, piece), bf16),
            pltpu.VMEM((2 * PARTS, 4, rows, piece), bf16),
            pltpu.VMEM((PARTS, rows, piece), bf16),
            dma((8,)),
            dma((7 * CHUNKS,)),
            dma((NZ, CHUNKS)),
            dma((2, 7)),
            dma((2, NT)),
            dma((2 + heads,)),
            dma((2 + heads,)),
            dma((2 * PARTS, NT - 1)),
            dma((2 * PARTS, NT - 1)),
            dma((PARTS,)),
            dma((PARTS,)),
        ],
        compiler_params=pltpu.CompilerParams(
            collective_id=0, has_side_effects=True, vmem_limit_bytes=48 << 20
        ),
    )(
        pinned(hidden[0]),
        pinned(stale_kv[0]),
        pinned(jnp.transpose(w_qkv, (1, 0, 2))),
        pinned(w_out),
        pinned(jnp.transpose(mod_table, (1, 0, 2))),
        pinned(segment_ids.reshape(NP, slab)),
        pinned(step_index),
        pinned(guide_scale),
    )
    return branch_rows[None], guided


def solution(mesh):
    placed = (
        P("cfg", ("patch", "tensor"), None),
        P("cfg", None, "patch", "tensor"),
        P(None, None, "tensor"),
        P("tensor", None),
        P(),
        P(),
        P(),
        P(),
    )
    return jax.shard_map(
        body,
        mesh=mesh,
        in_specs=placed,
        out_specs=(P("cfg", ("patch", "tensor"), None), P(("patch", "tensor"), "cfg")),
        check_vma=False,
    )
```

time: 46.9 us -> 45.8 us (0.977)
  Pallas kernels: 44.9 us -> 43.8 us
    pallas_call x1, Pallas kernels: 44.9 us -> 43.8 us  [body(): pl.pallas_call(kernel, name='joint_attention', out_shape=(pltpu.VMEM((row...]
where the time goes in v3:
time: 45.8 us; the launch traced here: 45.7 us
  Pallas kernels  43.8 us (96%)
  local copies, waits for them, and re-layouts  1.26 us (3%)
  between operations  0.64 us (1%)
    pallas_call x1, Pallas kernels, body(): pl.pallas_call(kernel, name='joint_attention', out_shape=(pltpu.VMEM((row...  43.8 us
    unnamed x2, local copies, waits for them, and re-layouts  1.26 us

profile of v3, /device:TPU:1, one launch (start us, length us, event | category | flops | bytes accessed | tf_op | source)
XLA Modules:
  0.0 45.7 jit_solution(13457995651220396179)
XLA Ops:
  0.6 43.8 %joint_attention.1 = (bf16[16,3072]{1,0:T(8,128)(2,1)S(1)}, bf16[16,1536]{1,0:T(8,128)(2,1)S(1)}) custom-call(bf16[16,3072]{1,0:T(8,128)(2,1)} %bitcast.10, bf16[2,128,384]{2,1,0:T(8,128)(2,1)} %bitcast.9, bf16[3,3072,384]{2,1,0:T(8,128)(2,1)} %bitcast.7, bf16[384,3072]{1,0:T(8,128)(2,1)} %w_out.1, f32[3,32,3072]{2,1,0:T(8,128)} %bitcast.8, ...), custom_call_target="tpu_custom_call" | custom-call | tf_op jit(solution)/shard_map/joint_attention/pallas_call | solution.py:448
  44.4 0.6 %copy.12 = bf16[1,16,3072]{2,1,0:T(8,128)(2,1)} copy(bf16[1,16,3072]{2,1,0:T(8,128)(2,1)S(1)} %bitcast.6) | data formatting | bytes 196608
  45.0 0.6 %copy.13 = bf16[16,1536]{1,0:T(8,128)(2,1)} copy(bf16[16,1536]{1,0:T(8,128)(2,1)S(1)} %get-tuple-element.7) | data formatting | bytes 98304

commit v4 on v3

--- a/solution.py
+++ b/solution.py
@@ -235,10 +235,12 @@
         take(-d, c)
         take(d, swap(c))
 
-    for part in range(2):
-        relay_tokens(part)
-        for c in range(part * CHUNKS // 2, (part + 1) * CHUNKS // 2):
-            take_both(1, c)
+    for c in range(CHUNKS // 2):
+        take_both(1, c)
+    relay_tokens(0)
+    relay_tokens(1)
+    for c in range(CHUNKS // 2, CHUNKS):
+        take_both(1, c)
     fill_bias(0, query_segs[...])
     fill_bias(1, column(z * 2 + (1 - yh)))
     for c in range(CHUNKS):
@@ -381,6 +383,9 @@
                 sum_recv.at[part, index],
                 to,
             )
+    for copy in sent[:-8 * PARTS]:
+        copy.wait_send()
+    del sent[: -8 * PARTS]
     strength = jnp.zeros((rows, LANES), jnp.float32)
     for r in range(8):
         strength = jnp.where(own_segs == r, strengths[r], strength)

time: 45.8 us -> 45.8 us (level)
  no operation moved by 1% of the time
where the time goes in v4:
time: 45.8 us; the launch traced here: 45.7 us
  Pallas kernels  43.8 us (96%)
  local copies, waits for them, and re-layouts  1.26 us (3%)
  between operations  0.64 us (1%)
    pallas_call x1, Pallas kernels, body(): pl.pallas_call(kernel, name='joint_attention', out_shape=(pltpu.VMEM((row...  43.8 us
    unnamed x2, local copies, waits for them, and re-layouts  1.26 us

profile of v4, /device:TPU:1, one launch (start us, length us, event | category | flops | bytes accessed | tf_op | source)
XLA Modules:
  0.0 45.7 jit_solution(1242841426792746529)
XLA Ops:
  0.6 43.8 %joint_attention.1 = (bf16[16,3072]{1,0:T(8,128)(2,1)S(1)}, bf16[16,1536]{1,0:T(8,128)(2,1)S(1)}) custom-call(bf16[16,3072]{1,0:T(8,128)(2,1)} %bitcast.10, bf16[2,128,384]{2,1,0:T(8,128)(2,1)} %bitcast.9, bf16[3,3072,384]{2,1,0:T(8,128)(2,1)} %bitcast.7, bf16[384,3072]{1,0:T(8,128)(2,1)} %w_out.1, f32[3,32,3072]{2,1,0:T(8,128)} %bitcast.8, ...), custom_call_target="tpu_custom_call" | custom-call | tf_op jit(solution)/shard_map/joint_attention/pallas_call | solution.py:453
  44.4 0.6 %copy.12 = bf16[1,16,3072]{2,1,0:T(8,128)(2,1)} copy(bf16[1,16,3072]{2,1,0:T(8,128)(2,1)S(1)} %bitcast.6) | data formatting | bytes 196608
  45.1 0.6 %copy.13 = bf16[16,1536]{1,0:T(8,128)(2,1)} copy(bf16[16,1536]{1,0:T(8,128)(2,1)S(1)} %get-tuple-element.7) | data formatting | bytes 98304

commit v5 on v4

--- a/solution.py
+++ b/solution.py
@@ -105,7 +105,7 @@
         pltpu.make_async_copy(w_out, wo, local_sem.at[4]),
         pltpu.make_async_copy(stale, kv.at[0], local_sem.at[5]),
     ]
-    for load in loads[:5]:
+    for load in loads:
         load.start()
 
     sent = []
@@ -223,8 +223,6 @@
         send_tokens(0, 0, 0, 1, 2, part)
     for part in range(2):
         send_tokens(0, 0, 2, 0, 3, part)
-    for load in loads[5:]:
-        load.start()
 
     def fill_bias(which, seg_column):
         for d in range(NZ):
@@ -311,9 +309,6 @@
     arrived(far_queries, far_recv.at[0], far_send.at[0])
     loads[7].wait()
     far = meet(1, far_queries, early)
-    for j in (KEY, VAL):
-        kv[0, j] = fresh_kv[j]
-    own = meet(0, queries, early)
     for c in range(CHUNKS // 2):
         take(4, c)
         take(4, swap(c))
@@ -334,8 +329,9 @@
         packed = jnp.where(lane == heads + head, total, packed)
     stats[...] = packed.T[:8]
     send(stats, stats_back, far_send.at[1 + heads], far_recv.at[1 + heads], across)
-    own_late = meet(0, queries, late)
-    own = [merge(own[head], own_late[head]) for head in range(heads)]
+    for j in (KEY, VAL):
+        kv[0, j] = fresh_kv[j]
+    own = meet(0, queries, ((0, 2), (2, 2), (4, 2), (6, 2)))
 
     arrived(stats_back, far_recv.at[1 + heads], far_send.at[0])
     back = jnp.concatenate([stats_back[...]] * (LANES // 8), axis=0).T

time: 45.8 us -> 45.6 us (level)
  no operation moved by 1% of the time
where the time goes in v5:
time: 45.6 us; the launch traced here: 45.5 us
  Pallas kernels  43.6 us (96%)
  local copies, waits for them, and re-layouts  1.26 us (3%)
  between operations  0.64 us (1%)
    pallas_call x1, Pallas kernels, body(): pl.pallas_call(kernel, name='joint_attention', out_shape=(pltpu.VMEM((row...  43.6 us
    unnamed x2, local copies, waits for them, and re-layouts  1.26 us

profile of v5, /device:TPU:1, one launch (start us, length us, event | category | flops | bytes accessed | tf_op | source)
XLA Modules:
  0.0 45.5 jit_solution(2772363540034514946)
XLA Ops:
  0.6 43.6 %joint_attention.1 = (bf16[16,3072]{1,0:T(8,128)(2,1)S(1)}, bf16[16,1536]{1,0:T(8,128)(2,1)S(1)}) custom-call(bf16[16,3072]{1,0:T(8,128)(2,1)} %bitcast.10, bf16[2,128,384]{2,1,0:T(8,128)(2,1)} %bitcast.9, bf16[3,3072,384]{2,1,0:T(8,128)(2,1)} %bitcast.7, bf16[384,3072]{1,0:T(8,128)(2,1)} %w_out.1, f32[3,32,3072]{2,1,0:T(8,128)} %bitcast.8, ...), custom_call_target="tpu_custom_call" | custom-call | tf_op jit(solution)/shard_map/joint_attention/pallas_call | solution.py:449
  44.2 0.6 %copy.12 = bf16[1,16,3072]{2,1,0:T(8,128)(2,1)} copy(bf16[1,16,3072]{2,1,0:T(8,128)(2,1)S(1)} %bitcast.6) | data formatting | bytes 196608
  44.9 0.6 %copy.13 = bf16[16,1536]{1,0:T(8,128)(2,1)} copy(bf16[16,1536]{1,0:T(8,128)(2,1)S(1)} %get-tuple-element.7) | data formatting | bytes 98304

commit v6 on v5

--- a/solution.py
+++ b/solution.py
@@ -44,7 +44,6 @@
     wo,
     tokens,
     kv,
-    fresh_kv,
     queries,
     far_queries,
     bias,
@@ -253,11 +252,6 @@
     send(queries, far_queries, far_send.at[0], far_recv.at[0], across)
     for c in range(CHUNKS):
         take_both(3, c)
-    for j in (KEY, VAL):
-        fresh_kv[j] = jnp.dot(
-            tokens[...], wq[1 + j], preferred_element_type=jnp.float32
-        ).astype(jnp.bfloat16)
-
     scale = math.log2(math.e) / HEAD_DIM**0.5
 
     def meet(which, q_ref, runs):
@@ -330,7 +324,9 @@
     stats[...] = packed.T[:8]
     send(stats, stats_back, far_send.at[1 + heads], far_recv.at[1 + heads], across)
     for j in (KEY, VAL):
-        kv[0, j] = fresh_kv[j]
+        kv[0, j] = jnp.dot(
+            tokens[...], wq[1 + j], preferred_element_type=jnp.float32
+        ).astype(jnp.bfloat16)
     own = meet(0, queries, ((0, 2), (2, 2), (4, 2), (6, 2)))
 
     arrived(stats_back, far_recv.at[1 + heads], far_send.at[0])
@@ -469,7 +465,6 @@
             pltpu.VMEM((local, width), bf16),
             pltpu.VMEM((slab, width), bf16),
             pltpu.VMEM((NZ, 2, slab, local), bf16),
-            pltpu.VMEM((2, slab, local), bf16),
             pltpu.VMEM((slab, local), bf16),
             pltpu.VMEM((slab, local), bf16),
             pltpu.VMEM((2, slab, NZ * slab), f32),

time: 45.6 us -> 45.1 us (0.989)
  Pallas kernels: 43.6 us -> 43.1 us
    pallas_call x1, Pallas kernels: 43.6 us -> 43.1 us  [body(): pl.pallas_call(kernel, name='joint_attention', out_shape=(pltpu.VMEM((row...]
where the time goes in v6:
time: 45.1 us; the launch traced here: 45 us
  Pallas kernels  43.1 us (96%)
  local copies, waits for them, and re-layouts  1.26 us (3%)
  between operations  0.64 us (1%)
    pallas_call x1, Pallas kernels, body(): pl.pallas_call(kernel, name='joint_attention', out_shape=(pltpu.VMEM((row...  43.1 us
    unnamed x2, local copies, waits for them, and re-layouts  1.26 us

profile of v6, /device:TPU:1, one launch (start us, length us, event | category | flops | bytes accessed | tf_op | source)
XLA Modules:
  0.0 45.0 jit_solution(9692165090729770110)
XLA Ops:
  0.6 43.1 %joint_attention.1 = (bf16[16,3072]{1,0:T(8,128)(2,1)S(1)}, bf16[16,1536]{1,0:T(8,128)(2,1)S(1)}) custom-call(bf16[16,3072]{1,0:T(8,128)(2,1)} %bitcast.10, bf16[2,128,384]{2,1,0:T(8,128)(2,1)} %bitcast.9, bf16[3,3072,384]{2,1,0:T(8,128)(2,1)} %bitcast.7, bf16[384,3072]{1,0:T(8,128)(2,1)} %w_out.1, f32[3,32,3072]{2,1,0:T(8,128)} %bitcast.8, ...), custom_call_target="tpu_custom_call" | custom-call | tf_op jit(solution)/shard_map/joint_attention/pallas_call | solution.py:445
  43.7 0.6 %copy.12 = bf16[1,16,3072]{2,1,0:T(8,128)(2,1)} copy(bf16[1,16,3072]{2,1,0:T(8,128)(2,1)S(1)} %bitcast.6) | data formatting | bytes 196608
  44.4 0.6 %copy.13 = bf16[16,1536]{1,0:T(8,128)(2,1)} copy(bf16[16,1536]{1,0:T(8,128)(2,1)S(1)} %get-tuple-element.7) | data formatting | bytes 98304
